TPU v7x, 32 devices: a whole 2x2x4 slice. The times are simulated.
32 devices in a mesh: parts: 2 (over y), rows: 16 (over z, x, core).
Axes of the slice: x: 2, y: 2, z: 4, core: 2. Of those that a mesh axis runs over, the one named last changes fastest.
Arguments:
- features: bfloat16 [12288, 1024], P(('parts', 'rows')), parts along dimension 0, may hold values from -6 to 6
- w_self: bfloat16 [2, 1024, 1024], replicated, may hold values from -0.1875 to 0.1875
- w_neigh: bfloat16 [2, 1024, 1024], replicated, may hold values from -0.1875 to 0.1875
- requests: int32 [512, 8], P(('parts', 'rows')), parts along dimension 0, may hold values from 0 to 383
- counts: int32 [512], P(('parts', 'rows')), parts along dimension 0, may hold values from 0 to 8, as said below
- mask_remote: int32 [12288, 128], P(('parts', 'rows')), parts along dimension 0, may hold values 0 or 1
- mask_local: int32 [12288, 384], P(('parts', 'rows')), parts along dimension 0, may hold values 0 or 1
Outputs:
- embeddings: bfloat16 [12288, 1024], P(('parts', 'rows')), parts along dimension 0
There are 2 independent parts, one for each index of `parts`. A program takes and returns all parts, laid end to end along the dimension named above; an argument that names none is the same for every part. Nothing has to cross between parts.
Inputs may be any that keep to these rules, and one draw needn't show every extreme that they name: `counts`: for each requesting device at least one owner's count is exactly 8.
All inputs are finite; a program needn't handle non-finite values. No bound on the sum of `mask_remote` or of `mask_local` on one device may be relied on, other than what follows from the above.
Results may differ from a plain program's by a relative error of at most 0.0047.
Values may be sent and summed in bfloat16 or wider, within the bound.
A program may use at most 64 MiB of HBM per device.

v0:
```python
import jax
import jax.numpy as jnp
from jax import lax
from jax.sharding import PartitionSpec as P


def shards(features, w_self, w_neigh, requests, counts, mask_remote, mask_local):
    devices = lax.axis_size("rows")
    slots = requests.shape[1]
    width = features.shape[1]
    wanted = lax.all_to_all(requests, "rows", split_axis=0, concat_axis=0, tiled=True)
    flat_rows = wanted.reshape(-1)
    valid = (
        (jnp.arange(slots, dtype=jnp.int32)[None, :] < counts[:, None])
        .astype(jnp.int32)
        .reshape(-1)
    )
    remote_int = mask_remote * valid[None, :]
    degree = (
        1.0
        + jnp.sum(remote_int, axis=1).astype(jnp.float32)
        + jnp.sum(mask_local, axis=1).astype(jnp.float32)
    )
    remote_edges = remote_int.astype(jnp.bfloat16)
    local_edges = mask_local.astype(jnp.bfloat16)
    hidden = features
    for layer in range(w_self.shape[0]):
        proj = jnp.dot(hidden, w_neigh[layer], preferred_element_type=jnp.float32).astype(
            jnp.bfloat16
        )
        outgoing = proj[flat_rows].reshape(devices, slots, width)
        fetched = lax.all_to_all(outgoing, "rows", split_axis=0, concat_axis=0, tiled=True).reshape(
            devices * slots, width
        )
        self_part = jnp.dot(hidden, w_self[layer], preferred_element_type=jnp.float32)
        total = proj.astype(jnp.float32) + jnp.dot(
            local_edges, proj, preferred_element_type=jnp.float32
        )
        total = total + jnp.dot(remote_edges, fetched, preferred_element_type=jnp.float32)
        pre = self_part + total / degree[:, None]
        act = jnp.maximum(pre, 0.0)
        scale = jnp.sqrt(jnp.mean(act * act, axis=1, keepdims=True) + 1e-05)
        hidden = (act / scale).astype(jnp.bfloat16)
    return hidden


def solution(mesh):
    in_specs = (
        P(("parts", "rows"), None),
        P(),
        P(),
        P(("parts", "rows"), None),
        P(("parts", "rows")),
        P(("parts", "rows"), None),
        P(("parts", "rows"), None),
    )
    out_specs = P(("parts", "rows"), None)
    return jax.shard_map(shards, mesh=mesh, in_specs=in_specs, out_specs=out_specs, check_vma=False)
```

profile of v0, /device:TPU:0, one launch (start us, length us, event | category | flops | bytes accessed | tf_op | source)
XLA Modules:
  0.0 55.3 jit_solution(7047590554924009846)
XLA Ops:
  0.0 0.0 copy-start
  0.0 1.4 %copy.15 = s32[16,1,8]{2,1,0:T(1,128)} copy(s32[16,1,8]{0,2,1:T(8,128)} %bitcast.51) | data formatting | bytes 1024 | tf_op jit(solution)/shard_map/all_to_all | solution.py:11
  1.4 7.4 %all-to-all-start = ((s32[16,1,8]{2,1,0:T(1,128)}), s32[16,1,8]{2,1,0:T(1,128)S(1)}, u32[]{:S(2)}, u32[]{:S(2)}) async-start(s32[16,1,8]{2,1,0:T(1,128)} %copy.15), calls=%async_computation | async-start | bytes 16384 | tf_op jit(solution)/shard_map/all_to_all | solution.py:11
  8.8 0.7 %fusion.32 = s32[16,8]{1,0:T(8,128)S(1)} fusion(s32[16]{0:T(128)} %param.11), kind=kLoop, calls=%fused_computation.39 | loop fusion | flops 256 | bytes 576 | tf_op jit(solution)/shard_map/convert_element_type | solution.py:15
  9.5 0.1 reshape.93
  9.6 0.0 copy-start.1
  9.6 0.0 copy-start.2
  9.6 2.6 %fusion.20 = bf16[384,1024]{1,0:T(8,128)(2,1)S(1)} fusion(bf16[384,1024]{1,0:T(8,128)(2,1)S(1)} %copy-done, bf16[2,1024,1024]{2,1,0:T(8,128)(2,1)} %param.9), kind=kOutput, calls=%fused_computation.28 | convolution fusion | flops 805699584 | bytes 3670016 | tf_op jit(solution)/shard_map/dot_general | solution.py:28
  12.3 0.1 multiply_reduce_fusion.2
  12.5 0.1 reduce_sum.37
  12.6 2.5 %all-to-all-done = s32[16,1,8]{2,1,0:T(1,128)S(1)} async-done(((s32[16,1,8]{2,1,0:T(1,128)}), s32[16,1,8]{2,1,0:T(1,128)S(1)}, u32[]{:S(2)}, u32[]{:S(2)}) %all-to-all-start) | async-done | bytes 544 | tf_op jit(solution)/shard_map/all_to_all | solution.py:11
  15.1 0.5 broadcast.82
  15.6 0.7 %reduce.3 = s32[16,8]{1,0:T(8,128)S(1)} reduce(s32[16,1,8]{2,1,0:T(1,128)S(1)} %all-to-all-done, s32[]{:T(128)} %broadcast.82), dimensions={1}, to_apply=%all_to_all.13.reduce_sub_computation.3 | reduce | bytes 1028 | tf_op jit(solution)/shard_map/all_to_all | solution.py:11
  16.3 0.1 reshape.88
  16.4 1.6 %gather_fusion = bf16[128,1024]{1,0:T(8,128)(2,1)} fusion(bf16[384,1024]{1,0:T(8,128)(2,1)S(1)} %fusion.20, s32[1024]{0:T(1024)S(1)} %pad_clamp_fusion), kind=kCustom, calls=%fused_computation | custom fusion | bytes 524800 | tf_op jit(solution)/shard_map/gather | solution.py:31
  18.0 3.5 %all-to-all-start.1 = ((bf16[16,8,1024]{2,1,0:T(8,128)(2,1)}), bf16[16,8,1024]{2,1,0:T(8,128)(2,1)S(1)}, u32[]{:S(2)}, u32[]{:S(2)}) async-start(bf16[16,8,1024]{2,1,0:T(8,128)(2,1)} %bitcast.5), calls=%async_computation.1 | async-start | bytes 524288 | tf_op jit(solution)/shard_map/all_to_all | solution.py:32
  21.5 3.7 %fusion.6 = f32[384,1024]{1,0:T(8,128)} fusion(bf16[384,1024]{1,0:T(8,128)(2,1)S(1)} %copy-done, bf16[2,1024,1024]{2,1,0:T(8,128)(2,1)} %param.8), kind=kOutput, calls=%fused_computation.8 | convolution fusion | flops 805306368 | bytes 4456448 | tf_op jit(solution)/shard_map/dot_general | solution.py:35
  25.3 6.3 %all-to-all-done.1 = bf16[16,8,1024]{2,1,0:T(8,128)(2,1)S(1)} async-done(((bf16[16,8,1024]{2,1,0:T(8,128)(2,1)}), bf16[16,8,1024]{2,1,0:T(8,128)(2,1)S(1)}, u32[]{:S(2)}, u32[]{:S(2)}) %all-to-all-start.1) | async-done | bytes 262176 | tf_op jit(solution)/shard_map/all_to_all | solution.py:32
  31.5 0.3 fusion.28
  31.9 1.1 %copy-done.4 = f32[384,1024]{1,0:T(8,128)S(1)} copy-done((f32[384,1024]{1,0:T(8,128)S(1)}, f32[384,1024]{1,0:T(8,128)}, u32[]{:S(2)}) %copy-start.4) | copy-done | bytes 1572888
  33.0 0.9 %multiply_reduce_fusion.1 = (f32[384]{0:T(512)S(1)}, f32[384,1024]{1,0:T(8,128)S(1)}) fusion(f32[384,1024]{1,0:T(8,128)S(1)} %copy-done.4, f32[384]{0:T(512)S(1)} %convert_add_fusion, f32[384,1024]{1,0:T(8,128)S(1)} %fusion.28, bf16[384,1024]{1,0:T(8,128)(2,1)S(1)} %fusion.20, s32[384,384]{1,0:T(8,128)S(1)} %copy-done.2), kind=kOutput, calls=%fused_computation.27 | convolution fusion | flops 305282688 | bytes 6097920 | tf_op jit(solution)/shard_map/dot_general | solution.py:36
  33.9 1.1 %copy-done.5 = f32[384,1024]{1,0:T(8,128)} copy-done((f32[384,1024]{1,0:T(8,128)}, f32[384,1024]{1,0:T(8,128)S(1)}, u32[]{:S(2)}) %copy-start.5) | copy-done | bytes 1572888
  35.1 0.7 %copy-done.3 = bf16[2,1024,1024]{2,1,0:T(8,128)(2,1)S(1)} copy-done((bf16[2,1024,1024]{2,1,0:T(8,128)(2,1)S(1)}, bf16[2,1024,1024]{2,1,0:T(8,128)(2,1)}, u32[]{:S(2)}) %copy-start.3) | copy-done | bytes 4194328
  35.7 1.0 %fusion.23 = bf16[384,1024]{1,0:T(8,128)(2,1)S(1)} fusion(bf16[2,1024,1024]{2,1,0:T(8,128)(2,1)S(1)} %copy-done.3, f32[384,1024]{1,0:T(8,128)S(1)} %get-tuple-element.6, f32[384]{0:T(512)S(1)} %add_sqrt_fusion.1), kind=kOutput, calls=%fused_computation.29 | convolution fusion | flops 806486016 | bytes 4458496 | tf_op jit(solution)/shard_map/dot_general | solution.py:28
  36.7 1.6 %gather_fusion.1 = bf16[128,1024]{1,0:T(8,128)(2,1)} fusion(bf16[384,1024]{1,0:T(8,128)(2,1)S(1)} %fusion.23, s32[1024]{0:T(1024)S(1)} %pad_clamp_fusion), kind=kCustom, calls=%fused_computation.1 | custom fusion | bytes 524800 | tf_op jit(solution)/shard_map/gather | solution.py:31
  38.3 3.5 %all-to-all-start.2 = ((bf16[16,8,1024]{2,1,0:T(8,128)(2,1)}), bf16[16,8,1024]{2,1,0:T(8,128)(2,1)S(1)}, u32[]{:S(2)}, u32[]{:S(2)}) async-start(bf16[16,8,1024]{2,1,0:T(8,128)(2,1)} %bitcast.10), calls=%async_computation.2 | async-start | bytes 524288 | tf_op jit(solution)/shard_map/all_to_all | solution.py:32
  41.9 4.3 %fusion.2 = f32[384,1024]{1,0:T(8,128)} fusion(bf16[2,1024,1024]{2,1,0:T(8,128)(2,1)} %param.8, f32[384,1024]{1,0:T(8,128)} %copy-done.5, f32[384]{0:T(512)S(1)} %add_sqrt_fusion.1), kind=kOutput, calls=%fused_computation.4 | convolution fusion | flops 806092800 | bytes 5244416 | tf_op jit(solution)/shard_map/dot_general | solution.py:35
  46.1 5.8 %all-to-all-done.2 = bf16[16,8,1024]{2,1,0:T(8,128)(2,1)S(1)} async-done(((bf16[16,8,1024]{2,1,0:T(8,128)(2,1)}), bf16[16,8,1024]{2,1,0:T(8,128)(2,1)S(1)}, u32[]{:S(2)}, u32[]{:S(2)}) %all-to-all-start.2) | async-done | bytes 262176 | tf_op jit(solution)/shard_map/all_to_all | solution.py:32
  51.9 0.4 fusion.26
  52.2 1.0 %copy-done.6 = f32[384,1024]{1,0:T(8,128)S(1)} copy-done((f32[384,1024]{1,0:T(8,128)S(1)}, f32[384,1024]{1,0:T(8,128)}, u32[]{:S(2)}) %copy-start.6) | copy-done | bytes 1572888
  53.3 0.9 %multiply_reduce_fusion = (f32[384]{0:T(512)S(1)}, f32[384,1024]{1,0:T(8,128)S(1)}) fusion(f32[384,1024]{1,0:T(8,128)S(1)} %copy-done.6, f32[384]{0:T(512)S(1)} %convert_add_fusion, f32[384,1024]{1,0:T(8,128)S(1)} %fusion.26, bf16[384,1024]{1,0:T(8,128)(2,1)S(1)} %fusion.23, s32[384,384]{1,0:T(8,128)S(1)} %copy-done.2), kind=kOutput, calls=%fused_computation.25 | convolution fusion | flops 305282688 | bytes 6097920 | tf_op jit(solution)/shard_map/dot_general | solution.py:36
  54.2 1.1 %divide_convert_fusion = bf16[384,1024]{1,0:T(8,128)(2,1)} fusion(f32[384,1024]{1,0:T(8,128)S(1)} %get-tuple-element.8, f32[384]{0:T(512)S(1)} %add_sqrt_fusion), kind=kLoop, calls=%fused_computation.24 | loop fusion | flops 786432 | bytes 2360832 | tf_op jit(solution)/shard_map/convert_element_type | solution.py:43
  (12 shorter events, 0.0 us)
Async XLA Ops:
  0.0 9.6 %copy-start = (bf16[384,1024]{1,0:T(8,128)(2,1)S(1)}, bf16[384,1024]{1,0:T(8,128)(2,1)}, u32[]{:S(2)}) copy-start(bf16[384,1024]{1,0:T(8,128)(2,1)} %param.7) | copy-start | bytes 2359300
  1.4 13.7 %all-to-all-start = ((s32[16,1,8]{2,1,0:T(1,128)}), s32[16,1,8]{2,1,0:T(1,128)S(1)}, u32[]{:S(2)}, u32[]{:S(2)}) async-start(s32[16,1,8]{2,1,0:T(1,128)} %copy.15), calls=%async_computation | async-start | bytes 16384 | tf_op jit(solution)/shard_map/all_to_all | solution.py:11
  9.6 2.7 %copy-start.1 = (s32[384,128]{1,0:T(8,128)S(1)}, s32[384,128]{1,0:T(8,128)}, u32[]{:S(2)}) copy-start(s32[384,128]{1,0:T(8,128)} %param.12) | copy-start | bytes 589828
  9.6 2.8 %copy-start.2 = (s32[384,384]{1,0:T(8,128)S(1)}, s32[384,384]{1,0:T(8,128)}, u32[]{:S(2)}) copy-start(s32[384,384]{1,0:T(8,128)} %param.13) | copy-start | bytes 1769476
  18.0 13.6 %all-to-all-start.1 = ((bf16[16,8,1024]{2,1,0:T(8,128)(2,1)}), bf16[16,8,1024]{2,1,0:T(8,128)(2,1)S(1)}, u32[]{:S(2)}, u32[]{:S(2)}) async-start(bf16[16,8,1024]{2,1,0:T(8,128)(2,1)} %bitcast.5), calls=%async_computation.1 | async-start | bytes 524288 | tf_op jit(solution)/shard_map/all_to_all | solution.py:32
  31.5 1.4 %copy-start.4 = (f32[384,1024]{1,0:T(8,128)S(1)}, f32[384,1024]{1,0:T(8,128)}, u32[]{:S(2)}) copy-start(f32[384,1024]{1,0:T(8,128)} %fusion.6) | copy-start | bytes 4718596
  33.0 2.8 %copy-start.3 = (bf16[2,1024,1024]{2,1,0:T(8,128)(2,1)S(1)}, bf16[2,1024,1024]{2,1,0:T(8,128)(2,1)}, u32[]{:S(2)}) copy-start(bf16[2,1024,1024]{2,1,0:T(8,128)(2,1)} %param.9) | copy-start | bytes 12582916
  33.9 1.2 %copy-start.5 = (f32[384,1024]{1,0:T(8,128)}, f32[384,1024]{1,0:T(8,128)S(1)}, u32[]{:S(2)}) copy-start(f32[384,1024]{1,0:T(8,128)S(1)} %get-tuple-element.6) | copy-start | bytes 4718596
  38.3 13.5 %all-to-all-start.2 = ((bf16[16,8,1024]{2,1,0:T(8,128)(2,1)}), bf16[16,8,1024]{2,1,0:T(8,128)(2,1)S(1)}, u32[]{:S(2)}, u32[]{:S(2)}) async-start(bf16[16,8,1024]{2,1,0:T(8,128)(2,1)} %bitcast.10), calls=%async_computation.2 | async-start | bytes 524288 | tf_op jit(solution)/shard_map/all_to_all | solution.py:32
  51.9 1.4 %copy-start.6 = (f32[384,1024]{1,0:T(8,128)S(1)}, f32[384,1024]{1,0:T(8,128)}, u32[]{:S(2)}) copy-start(f32[384,1024]{1,0:T(8,128)} %fusion.2) | copy-start | bytes 4718596
where the time goes:
time: 55.9 us; the launch traced here: 55.3 us
  waiting for transfers between devices  14.5 us (26%)
  starting transfers between devices  14.4 us (26%)
  matrix products  14.2 us (25%)
  local copies, waits for them, and re-layouts  9.16 us (16%)
  other arithmetic  2.84 us (5%)
    all_to_all x2, waiting for transfers between devices, shards(): lax.all_to_all(outgoing, 'rows', split_axis=0, concat_axis=0, tiled=True)  12 us
    dot_general x2, matrix products, shards(): jnp.dot(hidden, w_self[layer], preferred_element_type=jnp.float32)  7.98 us
    all_to_all x1, starting transfers between devices, shards(): lax.all_to_all(requests, 'rows', split_axis=0, concat_axis=0, tiled=True)  7.36 us
    all_to_all x2, starting transfers between devices, shards(): lax.all_to_all(outgoing, 'rows', split_axis=0, concat_axis=0, tiled=True)  7.07 us
    unnamed x14, local copies, waits for them, and re-layouts  3.92 us
    dot_general x2, matrix products, shards(): jnp.dot(hidden, w_neigh[layer], preferred_element_type=jnp.float32)  3.67 us
    gather x2, local copies, waits for them, and re-layouts, shards(): outgoing = proj[flat_rows].reshape(devices, slots, width)  3.13 us
    all_to_all x1, waiting for transfers between devices, shards(): lax.all_to_all(requests, 'rows', split_axis=0, concat_axis=0, tiled=True)  2.52 us
  transfers between devices with their start and end apart: 3, of which 3 were waited for; matrix products, arithmetic and copies ran while one was open for 21% of the time, Pallas kernels for 0%

commit v1 on v0

v1 whole, which is shorter than its diff:
```python
import functools

import jax
import jax.numpy as jnp
from jax import lax
from jax.experimental import pallas as pl
from jax.experimental.pallas import tpu as pltpu
from jax.sharding import PartitionSpec as P

LANES = 128
CHUNK = 256


def dot(a, b):
    return jnp.dot(a, b, preferred_element_type=jnp.float32)


def kernel(
    n, layers, feat_hbm, ws_hbm, wn_hbm, req_ref, cnt_ref, mr_hbm, ml_hbm, out_ref,
    hid, ws, wn, mr, ml, req_send, req_recv, row_send, row_recv,
    adj, edges, onehot, inv, base, local_sem, send_sem, recv_sem,
):
    me = lax.axis_index("rows")
    nodes, width = out_ref.shape
    slots = req_ref.shape[1]
    fetched = n * slots
    half = width // 2

    loads = [
        pltpu.make_async_copy(feat_hbm, hid, local_sem.at[0]),
        pltpu.make_async_copy(mr_hbm, mr, local_sem.at[1]),
        pltpu.make_async_copy(ml_hbm, ml, local_sem.at[2]),
    ]
    weights = []
    for layer in range(layers):
        weights.append((
            pltpu.make_async_copy(wn_hbm.at[layer], wn.at[layer], local_sem.at[3 + 2 * layer]),
            pltpu.make_async_copy(ws_hbm.at[layer], ws.at[layer], local_sem.at[4 + 2 * layer]),
        ))
    barrier = pltpu.get_barrier_semaphore()

    def greet(k, carry):
        peer = lax.rem(me + k, n)
        pl.semaphore_signal(
            barrier, inc=1, device_id={"rows": peer}, device_id_type=pl.DeviceIdType.MESH
        )
        return carry

    lax.fori_loop(1, n, greet, 0)
    for copy in loads:
        copy.start()
    for pair in weights:
        for copy in pair:
            copy.start()

    eye = lax.broadcasted_iota(jnp.int32, (slots, slots), 0) == lax.broadcasted_iota(
        jnp.int32, (slots, slots), 1
    )
    for o in range(n):
        row = jnp.broadcast_to(req_ref[o : o + 1, :], (slots, slots))
        column = jnp.sum(jnp.where(eye, row, 0), axis=1, keepdims=True)
        req_send[o] = jnp.broadcast_to(column, (slots, LANES))
    req_recv[me] = req_send[me]
    pl.semaphore_wait(barrier, n - 1)

    def remote(phase, src, dst, peer, origin):
        return pltpu.make_async_remote_copy(
            src_ref=src.at[peer],
            dst_ref=dst.at[origin],
            send_sem=send_sem.at[phase, peer],
            recv_sem=recv_sem.at[phase, origin],
            device_id={"rows": peer},
            device_id_type=pl.DeviceIdType.MESH,
        )

    def send_all(phase, src, dst):
        def body(k, carry):
            remote(phase, src, dst, lax.rem(me + k, n), me).start()
            return carry

        lax.fori_loop(1, n, body, 0)

    def recv_all(phase, src, dst):
        def body(k, carry):
            peer = lax.rem(me + k, n)
            remote(phase, src, dst, peer, peer).wait_recv()
            return carry

        lax.fori_loop(1, n, body, 0)

    def sent_all(phase, src, dst):
        def body(k, carry):
            remote(phase, src, dst, lax.rem(me + k, n), me).wait_send()
            return carry

        lax.fori_loop(1, n, body, 0)

    send_all(0, req_send, req_recv)

    lane = lax.broadcasted_iota(jnp.int32, (1, fetched), 1)
    owner = lane // slots
    used = jnp.zeros((1, fetched), jnp.int32)
    for o in range(n):
        used = jnp.where(owner == o, cnt_ref[o], used)
    valid = (lane - owner * slots < used).astype(jnp.int32)
    loads[1].wait()
    loads[2].wait()
    remote_int = mr[...] * valid
    local_int = ml[...]
    edges[...] = remote_int.astype(jnp.float32).astype(jnp.bfloat16)
    diagonal = lax.broadcasted_iota(jnp.int32, (nodes, nodes), 0) == lax.broadcasted_iota(
        jnp.int32, (nodes, nodes), 1
    )
    adj[...] = (
        (local_int + diagonal.astype(jnp.int32)).astype(jnp.float32).astype(jnp.bfloat16)
    )
    degree = 1.0 + (
        jnp.sum(remote_int.astype(jnp.float32), axis=1, keepdims=True)
        + jnp.sum(local_int.astype(jnp.float32), axis=1, keepdims=True)
    )
    inv[...] = jnp.broadcast_to(1.0 / degree, (nodes, LANES))

    loads[0].wait()
    recv_all(0, req_send, req_recv)
    wanted = req_recv[...].reshape(fetched, LANES)
    lanes = lax.broadcasted_iota(jnp.int32, (fetched, LANES), 1)
    for c in range(nodes // LANES):
        onehot[:, c * LANES : (c + 1) * LANES] = (
            (wanted == lanes + c * LANES).astype(jnp.float32).astype(jnp.bfloat16)
        )

    for layer in range(layers):
        src, dst = row_send.at[layer], row_recv.at[layer]
        for part in range(2):
            picked = dot(onehot[...], hid[:, part * half : (part + 1) * half])
            for_peers = picked.reshape(n, slots, half)
            if part == 0:
                first = for_peers
            else:
                both = jnp.concatenate([first, for_peers], axis=1)
                row_send[layer] = both.astype(jnp.bfloat16)
        row_recv[layer, me] = row_send[layer, me]
        send_all(1 + layer, src, dst)

        for copy in weights[layer]:
            copy.wait()
        scale = jnp.concatenate([inv[...]] * (CHUNK // LANES), axis=1)
        for c in range(width // CHUNK):
            cols = slice(c * CHUNK, (c + 1) * CHUNK)
            proj = dot(hid[...], wn[layer, :, cols]).astype(jnp.bfloat16)
            base[:, cols] = dot(hid[...], ws[layer, :, cols]) + dot(adj[...], proj) * scale

        recv_all(1 + layer, src, dst)
        block = row_recv[layer].astype(jnp.float32)
        rows = jnp.concatenate(
            [block[:, :slots, :].reshape(fetched, half), block[:, slots:, :].reshape(fetched, half)],
            axis=1,
        ).astype(jnp.bfloat16)
        squares = jnp.zeros((nodes, LANES), jnp.float32)
        for c in range(width // CHUNK):
            cols = slice(c * CHUNK, (c + 1) * CHUNK)
            proj = dot(rows, wn[layer, :, cols]).astype(jnp.bfloat16)
            act = jnp.maximum(base[:, cols] + dot(edges[...], proj) * scale, 0.0)
            base[:, cols] = act
            for part in range(CHUNK // LANES):
                piece = act[:, part * LANES : (part + 1) * LANES]
                squares = squares + piece * piece
        mean = jnp.sum(squares, axis=1, keepdims=True) * (1.0 / width)
        norm = lax.rsqrt(mean + 1e-05)
        result = out_ref if layer == layers - 1 else hid
        for c in range(width // CHUNK):
            cols = slice(c * CHUNK, (c + 1) * CHUNK)
            result[:, cols] = (base[:, cols] * norm).astype(jnp.bfloat16)

    sent_all(0, req_send, req_recv)
    for layer in range(layers):
        sent_all(1 + layer, row_send.at[layer], row_recv.at[layer])


def shards(features, w_self, w_neigh, requests, counts, mask_remote, mask_local):
    n = lax.axis_size("rows")
    nodes, width = features.shape
    layers = w_self.shape[0]
    slots = requests.shape[1]
    fetched = n * slots
    flops = 2 * layers * nodes * width * (2 * width + nodes + fetched)
    hbm = pl.BlockSpec(memory_space=pl.ANY)
    return pl.pallas_call(
        functools.partial(kernel, n, layers),
        out_shape=jax.ShapeDtypeStruct((nodes, width), jnp.bfloat16),
        in_specs=[
            hbm, hbm, hbm,
            pl.BlockSpec(memory_space=pltpu.VMEM),
            pl.BlockSpec(memory_space=pltpu.SMEM),
            hbm, hbm,
        ],
        out_specs=pl.BlockSpec(memory_space=pltpu.VMEM),
        scratch_shapes=[
            pltpu.VMEM((nodes, width), jnp.bfloat16),
            pltpu.VMEM(w_self.shape, jnp.bfloat16),
            pltpu.VMEM(w_neigh.shape, jnp.bfloat16),
            pltpu.VMEM(mask_remote.shape, jnp.int32),
            pltpu.VMEM(mask_local.shape, jnp.int32),
            pltpu.VMEM((n, slots, LANES), jnp.int32),
            pltpu.VMEM((n, slots, LANES), jnp.int32),
            pltpu.VMEM((layers, n, 2 * slots, width // 2), jnp.bfloat16),
            pltpu.VMEM((layers, n, 2 * slots, width // 2), jnp.bfloat16),
            pltpu.VMEM((nodes, nodes), jnp.bfloat16),
            pltpu.VMEM((nodes, fetched), jnp.bfloat16),
            pltpu.VMEM((fetched, nodes), jnp.bfloat16),
            pltpu.VMEM((nodes, LANES), jnp.float32),
            pltpu.VMEM((nodes, width), jnp.float32),
            pltpu.SemaphoreType.DMA((3 + 2 * layers,)),
            pltpu.SemaphoreType.DMA((1 + layers, n)),
            pltpu.SemaphoreType.DMA((1 + layers, n)),
        ],
        compiler_params=pltpu.CompilerParams(
            collective_id=0, has_side_effects=True, vmem_limit_bytes=52 * 1024 * 1024
        ),
        cost_estimate=pl.CostEstimate(
            flops=flops, bytes_accessed=8 * width * width + 4 * nodes * width, transcendentals=0
        ),
    )(features, w_self, w_neigh, requests, counts, mask_remote, mask_local)


def solution(mesh):
    in_specs = (
        P(("parts", "rows"), None),
        P(),
        P(),
        P(("parts", "rows"), None),
        P(("parts", "rows")),
        P(("parts", "rows"), None),
        P(("parts", "rows"), None),
    )
    out_specs = P(("parts", "rows"), None)
    return jax.shard_map(shards, mesh=mesh, in_specs=in_specs, out_specs=out_specs, check_vma=False)
```

time: 55.9 us -> 32 us (0.57)
  the two profiles are of different devices: /device:TPU:0 before, /device:TPU:25 now
where the time goes in v1:
time: 32 us; the launch traced here: 31.6 us
  Pallas kernels  27.3 us (85%)
  local copies, waits for them, and re-layouts  4.28 us (13%)
    pallas_call x1, Pallas kernels, shards(): pl.pallas_call(functools.partial(kernel, n, layers), out_shape=jax.ShapeD...  27.3 us
    unnamed x8, local copies, waits for them, and re-layouts  4.28 us

profile of v1, /device:TPU:25, one launch (start us, length us, event | category | flops | bytes accessed | tf_op | source)
XLA Modules:
  0.0 31.6 jit_solution(17148514968755909110)
XLA Ops:
  0.0 0.8 %copy.8.req_ref = s32[16,8]{1,0:T(8,128)S(1)} copy(s32[16,8]{0,1:T(8,128)} %param.10) | data formatting | bytes 1024 | tf_op args[3]
  0.8 0.0 copy-start
  0.8 1.1 %copy-done = s32[384,384]{1,0:T(8,128)S(1)} copy-done((s32[384,384]{1,0:T(8,128)S(1)}, s32[384,384]{1,0:T(8,128)}, u32[]{:S(2)}) %copy-start) | copy-done | bytes 589848
  1.8 0.0 copy-start.1
  1.8 0.9 %copy-done.1 = s32[384,128]{1,0:T(8,128)S(1)} copy-done((s32[384,128]{1,0:T(8,128)S(1)}, s32[384,128]{1,0:T(8,128)}, u32[]{:S(2)}) %copy-start.1) | copy-done | bytes 196632
  2.8 0.0 copy-start.2
  2.8 0.7 %copy-done.2 = s32[16]{0:T(128)S(1)} copy-done((s32[16]{0:T(128)S(1)}, s32[16]{0:T(128)}, u32[]{:S(2)}) %copy-start.2) | copy-done | bytes 88
  3.4 27.3 %shard_map.73 = bf16[384,1024]{1,0:T(8,128)(2,1)S(1)} custom-call(bf16[384,1024]{1,0:T(8,128)(2,1)} %feat_hbm.1, bf16[2,1024,1024]{2,1,0:T(8,128)(2,1)} %ws_hbm.1, bf16[2,1024,1024]{2,1,0:T(8,128)(2,1)} %wn_hbm.1, s32[16,8]{1,0:T(8,128)S(1)} %copy.8.req_ref, s32[16]{0:T(128)S(1)} %copy-done.2, s32[384,128]{1,0:T(8,128)S(1)} %copy-done.1, s32[384,384]{1,0:T(8,128)S(1)} %copy-done), custom_call_target="tpu_custom_call" | custom-call | flops 4026531840 | bytes 9961472 | tf_op jit(solution)/shard_map/pallas_call | solution.py:188
  30.7 0.9 %copy.10 = bf16[384,1024]{1,0:T(8,128)(2,1)} copy(bf16[384,1024]{1,0:T(8,128)(2,1)S(1)} %shard_map.73) | data formatting | bytes 1572864
Async XLA Ops:
  0.8 1.1 %copy-start = (s32[384,384]{1,0:T(8,128)S(1)}, s32[384,384]{1,0:T(8,128)}, u32[]{:S(2)}) copy-start(s32[384,384]{1,0:T(8,128)} %ml_hbm.1) | copy-start | bytes 1769476
  1.8 0.9 %copy-start.1 = (s32[384,128]{1,0:T(8,128)S(1)}, s32[384,128]{1,0:T(8,128)}, u32[]{:S(2)}) copy-start(s32[384,128]{1,0:T(8,128)} %mr_hbm.1) | copy-start | bytes 589828
  2.8 0.7 %copy-start.2 = (s32[16]{0:T(128)S(1)}, s32[16]{0:T(128)}, u32[]{:S(2)}) copy-start(s32[16]{0:T(128)} %cnt_ref.1) | copy-start | bytes 196

commit v2 on v1

--- a/solution.py
+++ b/solution.py
@@ -16,26 +16,29 @@
 
 
 def kernel(
-    n, layers, feat_hbm, ws_hbm, wn_hbm, req_ref, cnt_ref, mr_hbm, ml_hbm, out_ref,
-    hid, ws, wn, mr, ml, req_send, req_recv, row_send, row_recv,
+    n, layers, feat_hbm, ws_hbm, wn_hbm, req_hbm, cnt_hbm, mr_hbm, ml_hbm, out_ref,
+    req_ref, cnt_ref, hid, ws, wn, mr, ml, req_send, req_recv, row_send, row_recv,
     adj, edges, onehot, inv, base, local_sem, send_sem, recv_sem,
 ):
     me = lax.axis_index("rows")
     nodes, width = out_ref.shape
-    slots = req_ref.shape[1]
+    slots = req_ref.shape[0]
     fetched = n * slots
     half = width // 2
+    unroll = n <= 16
 
     loads = [
-        pltpu.make_async_copy(feat_hbm, hid, local_sem.at[0]),
-        pltpu.make_async_copy(mr_hbm, mr, local_sem.at[1]),
-        pltpu.make_async_copy(ml_hbm, ml, local_sem.at[2]),
+        pltpu.make_async_copy(req_hbm, req_ref, local_sem.at[0]),
+        pltpu.make_async_copy(cnt_hbm, cnt_ref, local_sem.at[1]),
+        pltpu.make_async_copy(mr_hbm, mr, local_sem.at[2]),
+        pltpu.make_async_copy(ml_hbm, ml, local_sem.at[3]),
+        pltpu.make_async_copy(feat_hbm, hid, local_sem.at[4]),
     ]
     weights = []
     for layer in range(layers):
         weights.append((
-            pltpu.make_async_copy(wn_hbm.at[layer], wn.at[layer], local_sem.at[3 + 2 * layer]),
-            pltpu.make_async_copy(ws_hbm.at[layer], ws.at[layer], local_sem.at[4 + 2 * layer]),
+            pltpu.make_async_copy(wn_hbm.at[layer], wn.at[layer], local_sem.at[5 + 2 * layer]),
+            pltpu.make_async_copy(ws_hbm.at[layer], ws.at[layer], local_sem.at[6 + 2 * layer]),
         ))
     barrier = pltpu.get_barrier_semaphore()
 
@@ -46,20 +49,16 @@
         )
         return carry
 
-    lax.fori_loop(1, n, greet, 0)
+    lax.fori_loop(1, n, greet, 0, unroll=unroll)
     for copy in loads:
         copy.start()
     for pair in weights:
         for copy in pair:
             copy.start()
 
-    eye = lax.broadcasted_iota(jnp.int32, (slots, slots), 0) == lax.broadcasted_iota(
-        jnp.int32, (slots, slots), 1
-    )
+    loads[0].wait()
     for o in range(n):
-        row = jnp.broadcast_to(req_ref[o : o + 1, :], (slots, slots))
-        column = jnp.sum(jnp.where(eye, row, 0), axis=1, keepdims=True)
-        req_send[o] = jnp.broadcast_to(column, (slots, LANES))
+        req_send[o] = jnp.broadcast_to(req_ref[:, o : o + 1], (slots, LANES))
     req_recv[me] = req_send[me]
     pl.semaphore_wait(barrier, n - 1)
 
@@ -78,7 +77,7 @@
             remote(phase, src, dst, lax.rem(me + k, n), me).start()
             return carry
 
-        lax.fori_loop(1, n, body, 0)
+        lax.fori_loop(1, n, body, 0, unroll=unroll)
 
     def recv_all(phase, src, dst):
         def body(k, carry):
@@ -86,25 +85,26 @@
             remote(phase, src, dst, peer, peer).wait_recv()
             return carry
 
-        lax.fori_loop(1, n, body, 0)
+        lax.fori_loop(1, n, body, 0, unroll=unroll)
 
     def sent_all(phase, src, dst):
         def body(k, carry):
             remote(phase, src, dst, lax.rem(me + k, n), me).wait_send()
             return carry
 
-        lax.fori_loop(1, n, body, 0)
+        lax.fori_loop(1, n, body, 0, unroll=unroll)
 
     send_all(0, req_send, req_recv)
 
     lane = lax.broadcasted_iota(jnp.int32, (1, fetched), 1)
     owner = lane // slots
+    loads[1].wait()
     used = jnp.zeros((1, fetched), jnp.int32)
     for o in range(n):
         used = jnp.where(owner == o, cnt_ref[o], used)
     valid = (lane - owner * slots < used).astype(jnp.int32)
-    loads[1].wait()
     loads[2].wait()
+    loads[3].wait()
     remote_int = mr[...] * valid
     local_int = ml[...]
     edges[...] = remote_int.astype(jnp.float32).astype(jnp.bfloat16)
@@ -120,7 +120,7 @@
     )
     inv[...] = jnp.broadcast_to(1.0 / degree, (nodes, LANES))
 
-    loads[0].wait()
+    loads[4].wait()
     recv_all(0, req_send, req_recv)
     wanted = req_recv[...].reshape(fetched, LANES)
     lanes = lax.broadcasted_iota(jnp.int32, (fetched, LANES), 1)
@@ -184,18 +184,15 @@
     slots = requests.shape[1]
     fetched = n * slots
     flops = 2 * layers * nodes * width * (2 * width + nodes + fetched)
-    hbm = pl.BlockSpec(memory_space=pl.ANY)
+    hbm = pl.BlockSpec(memory_space=pltpu.HBM)
     return pl.pallas_call(
         functools.partial(kernel, n, layers),
-        out_shape=jax.ShapeDtypeStruct((nodes, width), jnp.bfloat16),
-        in_specs=[
-            hbm, hbm, hbm,
-            pl.BlockSpec(memory_space=pltpu.VMEM),
-            pl.BlockSpec(memory_space=pltpu.SMEM),
-            hbm, hbm,
-        ],
+        out_shape=pltpu.VMEM((nodes, width), jnp.bfloat16),
+        in_specs=[hbm] * 7,
         out_specs=pl.BlockSpec(memory_space=pltpu.VMEM),
         scratch_shapes=[
+            pltpu.VMEM((slots, n), jnp.int32),
+            pltpu.SMEM(counts.shape, jnp.int32),
             pltpu.VMEM((nodes, width), jnp.bfloat16),
             pltpu.VMEM(w_self.shape, jnp.bfloat16),
             pltpu.VMEM(w_neigh.shape, jnp.bfloat16),
@@ -210,17 +207,17 @@
             pltpu.VMEM((fetched, nodes), jnp.bfloat16),
             pltpu.VMEM((nodes, LANES), jnp.float32),
             pltpu.VMEM((nodes, width), jnp.float32),
-            pltpu.SemaphoreType.DMA((3 + 2 * layers,)),
+            pltpu.SemaphoreType.DMA((5 + 2 * layers,)),
             pltpu.SemaphoreType.DMA((1 + layers, n)),
             pltpu.SemaphoreType.DMA((1 + layers, n)),
         ],
         compiler_params=pltpu.CompilerParams(
-            collective_id=0, has_side_effects=True, vmem_limit_bytes=52 * 1024 * 1024
+            collective_id=0, has_side_effects=True, vmem_limit_bytes=56 * 1024 * 1024
         ),
         cost_estimate=pl.CostEstimate(
             flops=flops, bytes_accessed=8 * width * width + 4 * nodes * width, transcendentals=0
         ),
-    )(features, w_self, w_neigh, requests, counts, mask_remote, mask_local)
+    )(features, w_self, w_neigh, requests.T, counts, mask_remote, mask_local)
 
 
 def solution(mesh):

time: 32 us -> 27.5 us (0.86)
  local copies, waits for them, and re-layouts: 4.28 us -> 0.88 us
  Pallas kernels: 27.3 us -> 26.3 us
    unnamed x8 -> x1, local copies, waits for them, and re-layouts: 4.28 us -> 0.88 us
    pallas_call x1, Pallas kernels: 27.3 us -> 26.3 us  [shards(): pl.pallas_call(functools.partial(kernel, n, layers), out_shape=pltpu.VMEM...]
where the time goes in v2:
time: 27.5 us; the launch traced here: 27.2 us
  Pallas kernels  26.3 us (96%)
  local copies, waits for them, and re-layouts  0.88 us (3%)
    pallas_call x1, Pallas kernels, shards(): pl.pallas_call(functools.partial(kernel, n, layers), out_shape=pltpu.VMEM...  26.3 us
    unnamed x1, local copies, waits for them, and re-layouts  0.88 us

profile of v2, /device:TPU:25, one launch (start us, length us, event | category | flops | bytes accessed | tf_op | source)
XLA Modules:
  0.0 27.2 jit_solution(12166593963046687012)
XLA Ops:
  0.0 26.3 %shard_map.73 = bf16[384,1024]{1,0:T(8,128)(2,1)S(1)} custom-call(bf16[384,1024]{1,0:T(8,128)(2,1)} %feat_hbm.1, bf16[2,1024,1024]{2,1,0:T(8,128)(2,1)} %ws_hbm.1, bf16[2,1024,1024]{2,1,0:T(8,128)(2,1)} %wn_hbm.1, s32[8,16]{1,0:T(8,128)} %bitcast.1, s32[16]{0:T(128)} %cnt_hbm.1, s32[384,128]{1,0:T(8,128)} %mr_hbm.1, s32[384,384]{1,0:T(8,128)} %ml_hbm.1), custom_call_target="tpu_custom_call" | custom-call | flops 4026531840 | bytes 9961472 | tf_op jit(solution)/shard_map/pallas_call | solution.py:188
  26.3 0.9 %copy.9 = bf16[384,1024]{1,0:T(8,128)(2,1)} copy(bf16[384,1024]{1,0:T(8,128)(2,1)S(1)} %shard_map.73) | data formatting | bytes 1572864

commit v3 on v2

--- a/solution.py
+++ b/solution.py
@@ -8,7 +8,7 @@
 from jax.sharding import PartitionSpec as P
 
 LANES = 128
-CHUNK = 256
+CHUNK = 512
 
 
 def dot(a, b):
@@ -18,7 +18,7 @@
 def kernel(
     n, layers, feat_hbm, ws_hbm, wn_hbm, req_hbm, cnt_hbm, mr_hbm, ml_hbm, out_ref,
     req_ref, cnt_ref, hid, ws, wn, mr, ml, req_send, req_recv, row_send, row_recv,
-    adj, edges, onehot, inv, base, local_sem, send_sem, recv_sem,
+    adj, edges, onehot, inv, base, raw, local_sem, send_sem, recv_sem,
 ):
     me = lax.axis_index("rows")
     nodes, width = out_ref.shape
@@ -56,9 +56,13 @@
         for copy in pair:
             copy.start()
 
+    diag = lax.broadcasted_iota(jnp.int32, (slots, LANES), 0) == lax.broadcasted_iota(
+        jnp.int32, (slots, LANES), 1
+    )
     loads[0].wait()
     for o in range(n):
-        req_send[o] = jnp.broadcast_to(req_ref[:, o : o + 1], (slots, LANES))
+        column = jnp.broadcast_to(req_ref[:, o : o + 1], (slots, LANES))
+        req_send[o] = jnp.sum(jnp.where(diag, column, 0), axis=0, keepdims=True)
     req_recv[me] = req_send[me]
     pl.semaphore_wait(barrier, n - 1)
 
@@ -122,26 +126,27 @@
 
     loads[4].wait()
     recv_all(0, req_send, req_recv)
-    wanted = req_recv[...].reshape(fetched, LANES)
+    spread = jnp.broadcast_to(req_recv[...], (n, slots, LANES))
+    columns = jnp.sum(jnp.where(diag[None], spread, 0), axis=2, keepdims=True)
+    wanted = jnp.broadcast_to(columns, (n, slots, LANES)).reshape(fetched, LANES)
     lanes = lax.broadcasted_iota(jnp.int32, (fetched, LANES), 1)
     for c in range(nodes // LANES):
         onehot[:, c * LANES : (c + 1) * LANES] = (
             (wanted == lanes + c * LANES).astype(jnp.float32).astype(jnp.bfloat16)
         )
 
+    def send_rows(source, layer):
+        pieces = []
+        for part in range(2):
+            picked = dot(onehot[...], source[:, part * half : (part + 1) * half])
+            pieces.append(picked.reshape(n, slots, half))
+        row_send[layer] = jnp.concatenate(pieces, axis=1).astype(jnp.bfloat16)
+        row_recv[layer, me] = row_send[layer, me]
+        send_all(1 + layer, row_send.at[layer], row_recv.at[layer])
+
+    send_rows(hid, 0)
     for layer in range(layers):
         src, dst = row_send.at[layer], row_recv.at[layer]
-        for part in range(2):
-            picked = dot(onehot[...], hid[:, part * half : (part + 1) * half])
-            for_peers = picked.reshape(n, slots, half)
-            if part == 0:
-                first = for_peers
-            else:
-                both = jnp.concatenate([first, for_peers], axis=1)
-                row_send[layer] = both.astype(jnp.bfloat16)
-        row_recv[layer, me] = row_send[layer, me]
-        send_all(1 + layer, src, dst)
-
         for copy in weights[layer]:
             copy.wait()
         scale = jnp.concatenate([inv[...]] * (CHUNK // LANES), axis=1)
@@ -155,16 +160,27 @@
         rows = jnp.concatenate(
             [block[:, :slots, :].reshape(fetched, half), block[:, slots:, :].reshape(fetched, half)],
             axis=1,
-        ).astype(jnp.bfloat16)
+        )
+        if layer > 0:
+            row_mean = jnp.sum(rows * rows, axis=1, keepdims=True) * (1.0 / width)
+            row_norm = lax.rsqrt(row_mean + 1e-05)
+        rows = rows.astype(jnp.bfloat16)
         squares = jnp.zeros((nodes, LANES), jnp.float32)
         for c in range(width // CHUNK):
             cols = slice(c * CHUNK, (c + 1) * CHUNK)
-            proj = dot(rows, wn[layer, :, cols]).astype(jnp.bfloat16)
+            proj = dot(rows, wn[layer, :, cols])
+            if layer > 0:
+                proj = proj * row_norm
+            proj = proj.astype(jnp.bfloat16)
             act = jnp.maximum(base[:, cols] + dot(edges[...], proj) * scale, 0.0)
             base[:, cols] = act
+            if layer < layers - 1:
+                raw[:, cols] = act.astype(jnp.bfloat16)
             for part in range(CHUNK // LANES):
                 piece = act[:, part * LANES : (part + 1) * LANES]
                 squares = squares + piece * piece
+        if layer < layers - 1:
+            send_rows(raw, layer + 1)
         mean = jnp.sum(squares, axis=1, keepdims=True) * (1.0 / width)
         norm = lax.rsqrt(mean + 1e-05)
         result = out_ref if layer == layers - 1 else hid
@@ -198,8 +214,8 @@
             pltpu.VMEM(w_neigh.shape, jnp.bfloat16),
             pltpu.VMEM(mask_remote.shape, jnp.int32),
             pltpu.VMEM(mask_local.shape, jnp.int32),
-            pltpu.VMEM((n, slots, LANES), jnp.int32),
-            pltpu.VMEM((n, slots, LANES), jnp.int32),
+            pltpu.VMEM((n, 1, LANES), jnp.int32),
+            pltpu.VMEM((n, 1, LANES), jnp.int32),
             pltpu.VMEM((layers, n, 2 * slots, width // 2), jnp.bfloat16),
             pltpu.VMEM((layers, n, 2 * slots, width // 2), jnp.bfloat16),
             pltpu.VMEM((nodes, nodes), jnp.bfloat16),
@@ -207,6 +223,7 @@
             pltpu.VMEM((fetched, nodes), jnp.bfloat16),
             pltpu.VMEM((nodes, LANES), jnp.float32),
             pltpu.VMEM((nodes, width), jnp.float32),
+            pltpu.VMEM((nodes, width), jnp.bfloat16),
             pltpu.SemaphoreType.DMA((5 + 2 * layers,)),
             pltpu.SemaphoreType.DMA((1 + layers, n)),
             pltpu.SemaphoreType.DMA((1 + layers, n)),

time: 27.5 us -> 26.5 us (0.964)
  Pallas kernels: 26.3 us -> 25.4 us
    pallas_call x1, Pallas kernels: 26.3 us -> 25.4 us  [shards(): pl.pallas_call(functools.partial(kernel, n, layers), out_shape=pltpu.VMEM...]
where the time goes in v3:
time: 26.5 us; the launch traced here: 26.3 us
  Pallas kernels  25.4 us (96%)
  local copies, waits for them, and re-layouts  0.88 us (3%)
    pallas_call x1, Pallas kernels, shards(): pl.pallas_call(functools.partial(kernel, n, layers), out_shape=pltpu.VMEM...  25.4 us
    unnamed x1, local copies, waits for them, and re-layouts  0.88 us

profile of v3, /device:TPU:25, one launch (start us, length us, event | category | flops | bytes accessed | tf_op | source)
XLA Modules:
  0.0 26.3 jit_solution(10477001669256335552)
XLA Ops:
  0.0 25.4 %shard_map.73 = bf16[384,1024]{1,0:T(8,128)(2,1)S(1)} custom-call(bf16[384,1024]{1,0:T(8,128)(2,1)} %feat_hbm.1, bf16[2,1024,1024]{2,1,0:T(8,128)(2,1)} %ws_hbm.1, bf16[2,1024,1024]{2,1,0:T(8,128)(2,1)} %wn_hbm.1, s32[8,16]{1,0:T(8,128)} %bitcast.1, s32[16]{0:T(128)} %cnt_hbm.1, s32[384,128]{1,0:T(8,128)} %mr_hbm.1, s32[384,384]{1,0:T(8,128)} %ml_hbm.1), custom_call_target="tpu_custom_call" | custom-call | flops 4026531840 | bytes 9961472 | tf_op jit(solution)/shard_map/pallas_call | solution.py:204
  25.4 0.9 %copy.9 = bf16[384,1024]{1,0:T(8,128)(2,1)} copy(bf16[384,1024]{1,0:T(8,128)(2,1)S(1)} %shard_map.73) | data formatting | bytes 1572864

commit v4 on v3

--- a/solution.py
+++ b/solution.py
@@ -64,42 +64,6 @@
         column = jnp.broadcast_to(req_ref[:, o : o + 1], (slots, LANES))
         req_send[o] = jnp.sum(jnp.where(diag, column, 0), axis=0, keepdims=True)
     req_recv[me] = req_send[me]
-    pl.semaphore_wait(barrier, n - 1)
-
-    def remote(phase, src, dst, peer, origin):
-        return pltpu.make_async_remote_copy(
-            src_ref=src.at[peer],
-            dst_ref=dst.at[origin],
-            send_sem=send_sem.at[phase, peer],
-            recv_sem=recv_sem.at[phase, origin],
-            device_id={"rows": peer},
-            device_id_type=pl.DeviceIdType.MESH,
-        )
-
-    def send_all(phase, src, dst):
-        def body(k, carry):
-            remote(phase, src, dst, lax.rem(me + k, n), me).start()
-            return carry
-
-        lax.fori_loop(1, n, body, 0, unroll=unroll)
-
-    def recv_all(phase, src, dst):
-        def body(k, carry):
-            peer = lax.rem(me + k, n)
-            remote(phase, src, dst, peer, peer).wait_recv()
-            return carry
-
-        lax.fori_loop(1, n, body, 0, unroll=unroll)
-
-    def sent_all(phase, src, dst):
-        def body(k, carry):
-            remote(phase, src, dst, lax.rem(me + k, n), me).wait_send()
-            return carry
-
-        lax.fori_loop(1, n, body, 0, unroll=unroll)
-
-    send_all(0, req_send, req_recv)
-
     lane = lax.broadcasted_iota(jnp.int32, (1, fetched), 1)
     owner = lane // slots
     loads[1].wait()
@@ -123,6 +87,42 @@
         + jnp.sum(local_int.astype(jnp.float32), axis=1, keepdims=True)
     )
     inv[...] = jnp.broadcast_to(1.0 / degree, (nodes, LANES))
+
+    pl.semaphore_wait(barrier, n - 1)
+
+    def remote(phase, src, dst, peer, origin):
+        return pltpu.make_async_remote_copy(
+            src_ref=src.at[peer],
+            dst_ref=dst.at[origin],
+            send_sem=send_sem.at[phase, peer],
+            recv_sem=recv_sem.at[phase, origin],
+            device_id={"rows": peer},
+            device_id_type=pl.DeviceIdType.MESH,
+        )
+
+    def send_all(phase, src, dst):
+        def body(k, carry):
+            remote(phase, src, dst, lax.rem(me + k, n), me).start()
+            return carry
+
+        lax.fori_loop(1, n, body, 0, unroll=unroll)
+
+    def recv_all(phase, src, dst):
+        def body(k, carry):
+            peer = lax.rem(me + k, n)
+            remote(phase, src, dst, peer, peer).wait_recv()
+            return carry
+
+        lax.fori_loop(1, n, body, 0, unroll=unroll)
+
+    def sent_all(phase, src, dst):
+        def body(k, carry):
+            remote(phase, src, dst, lax.rem(me + k, n), me).wait_send()
+            return carry
+
+        lax.fori_loop(1, n, body, 0, unroll=unroll)
+
+    send_all(0, req_send, req_recv)
 
     loads[4].wait()
     recv_all(0, req_send, req_recv)

time: 26.5 us -> 26.5 us (level)
  no operation moved by 1% of the time
where the time goes in v4:
time: 26.5 us; the launch traced here: 26.3 us
  Pallas kernels  25.4 us (96%)
  local copies, waits for them, and re-layouts  0.88 us (3%)
    pallas_call x1, Pallas kernels, shards(): pl.pallas_call(functools.partial(kernel, n, layers), out_shape=pltpu.VMEM...  25.4 us
    unnamed x1, local copies, waits for them, and re-layouts  0.88 us

profile of v4, /device:TPU:25, one launch (start us, length us, event | category | flops | bytes accessed | tf_op | source)
XLA Modules:
  0.0 26.3 jit_solution(17523529382389237378)
XLA Ops:
  0.0 25.4 %shard_map.73 = bf16[384,1024]{1,0:T(8,128)(2,1)S(1)} custom-call(bf16[384,1024]{1,0:T(8,128)(2,1)} %feat_hbm.1, bf16[2,1024,1024]{2,1,0:T(8,128)(2,1)} %ws_hbm.1, bf16[2,1024,1024]{2,1,0:T(8,128)(2,1)} %wn_hbm.1, s32[8,16]{1,0:T(8,128)} %bitcast.1, s32[16]{0:T(128)} %cnt_hbm.1, s32[384,128]{1,0:T(8,128)} %mr_hbm.1, s32[384,384]{1,0:T(8,128)} %ml_hbm.1), custom_call_target="tpu_custom_call" | custom-call | flops 4026531840 | bytes 9961472 | tf_op jit(solution)/shard_map/pallas_call | solution.py:204
  25.4 0.9 %copy.9 = bf16[384,1024]{1,0:T(8,128)(2,1)} copy(bf16[384,1024]{1,0:T(8,128)(2,1)S(1)} %shard_map.73) | data formatting | bytes 1572864
